TPU v7x, 256 devices: a whole 4x4x8 slice. The times are simulated.
256 devices in a mesh: dp: 16 (over x, y), tensor: 16 (over z, core).
Axes of the slice: x: 4, y: 4, z: 8, core: 2. Of those that a mesh axis runs over, the one named last changes fastest.
Arguments:
- activations: bfloat16 [4096, 16384], P('dp', 'tensor'), may hold values from -6 to 6
- angles: float32 [14, 8192], P(None, 'tensor'), may hold values from -3.140625 to 3.140625
- clip_bits: int32 [256, 16384], P('dp', 'tensor'), may hold values from 0 to 65535, as said below
- codes: bfloat16 [16384, 10240], P('tensor', 'dp'), may hold values from -127 to 127, as said below
- exponents: int32 [10240], replicated, may hold values from -16 to -13
- cotangent: bfloat16 [4096, 10240], P('dp', 'tensor'), may hold values from -6 to 6
Outputs:
- input_grad: bfloat16 [4096, 16384], P('dp', 'tensor')
- angle_grad: float32 [14, 8192], P(None, 'tensor')
Inputs may be any that keep to these rules, and one draw needn't show every extreme that they name: Bit k (0 to 15) of clip_bits[w, i] is the clip mask of token 16 w + k at feature i; higher bits are zero. `codes`: every entry is a whole number.
All inputs are finite; a program needn't handle non-finite values.
Results may differ from a plain program's by a relative error of at most 0.003.
Values may be sent and summed in bfloat16 or wider, within the bound.
A program may use at most 128 MiB of HBM per device.

v0:
```python
import jax
import jax.numpy as jnp
from jax import lax
from jax.sharding import PartitionSpec as P


def partner(value, axis, apart):
    mask = 2**apart
    pairs = [(source, source ^ mask) for source in range(lax.axis_size(axis))]
    return lax.ppermute(value, axis, pairs)


def split_up(value, dim, count):
    shape = value.shape
    parts = value.reshape(*shape[:dim], count, shape[dim] // count, *shape[dim + 1 :])
    return jnp.moveaxis(parts, dim, 0)


def sent_and_summed(value, axis, dim):
    count = lax.axis_size(axis)
    parts = lax.all_to_all(split_up(value, dim, count), axis, 0, 0, tiled=True)
    return jnp.sum(parts, axis=0)


def copy_for_each(value, axis):
    copies = jnp.broadcast_to(value, (lax.axis_size(axis), *value.shape))
    return lax.all_to_all(copies, axis, split_axis=0, concat_axis=0, tiled=True)


def over_copies(value, axis):
    everything = copy_for_each(value, axis)
    return jnp.sum(everything, axis=0)


def unpack_mask(clip_bits, rows, width):
    shifts = jnp.arange(16, dtype=jnp.int32)
    bits = jnp.bitwise_and(jnp.right_shift(clip_bits[:, None, :], shifts[None, :, None]), 1)
    return bits.reshape(rows, width).astype(jnp.float32)


def section_terms(table, section, first, width):
    half = 1 << section
    index = first + jnp.arange(width, dtype=jnp.int32)
    pair = jnp.right_shift(index, section + 1) * half + jnp.bitwise_and(index, half - 1)
    theta = jnp.take(table[section], pair)
    lower = jnp.bitwise_and(index, half) == 0
    sign = jnp.where(lower, -1.0, 1.0).astype(jnp.float32)
    return (jnp.cos(theta), sign * jnp.sin(theta), sign, pair)


def local_partner(field, section):
    half = 1 << section
    column = jnp.arange(field.shape[1], dtype=jnp.int32)
    lower = jnp.bitwise_and(column, half) == 0
    return jnp.where(lower[None, :], jnp.roll(field, -half, axis=1), jnp.roll(field, half, axis=1))


def scatter_terms(term, pair, half_pairs):
    return jnp.zeros((half_pairs,), jnp.float32).at[pair].add(term)


def body(activations, angles, clip_bits, codes, exponents, cotangent):
    rows, width = activations.shape
    sections = angles.shape[0]
    share = angles.shape[1]
    half_pairs = share * lax.axis_size("tensor")
    local_count = width.bit_length() - 1
    place = lax.axis_index("tensor")
    table = lax.all_gather(angles, "tensor", axis=1, tiled=True)
    scale = jnp.exp2(exponents.astype(jnp.float32))
    full_cot = lax.all_gather(cotangent, "tensor", axis=1, tiled=True)
    weight_piece = (
        lax.all_gather(codes, "dp", axis=1, tiled=True).astype(jnp.float32) * scale[None, :]
    ).astype(jnp.bfloat16)
    projected = lax.dot_general(
        full_cot, weight_piece, (((1,), (1,)), ((), ())), preferred_element_type=jnp.float32
    )
    grad_rot = projected * unpack_mask(clip_bits, rows, width)
    first = place * width
    field = activations.astype(jnp.float32)
    stored = [None] * sections
    for section in range(sections):
        cosine, signed, sign, pair = section_terms(table, section, first, width)
        if section < local_count:
            other = local_partner(field, section)
        else:
            other = partner(field.astype(jnp.bfloat16), "tensor", section - local_count).astype(
                field.dtype
            )
            stored[section] = (field, other)
        field = cosine * field + signed * other
    grad = grad_rot
    terms_list = [None] * sections
    for section in reversed(range(sections)):
        cosine, signed, sign, pair = section_terms(table, section, first, width)
        if section < local_count:
            other = local_partner(field, section)
            grad_other = local_partner(grad, section)
            before = cosine * field - signed * other
        else:
            before, before_other = stored[section]
            other = cosine * before_other - signed * before
            grad_other = partner(grad, "tensor", section - local_count)
        terms_list[section] = scatter_terms(jnp.sum(sign * grad * other, axis=0), pair, half_pairs)
        grad = cosine * grad - signed * grad_other
        field = before
    input_grad = grad.astype(jnp.bfloat16)
    collected = jnp.stack(terms_list)
    partial_total = sent_and_summed(collected, "tensor", 1)
    angle_grad = over_copies(partial_total, "dp")
    return (input_grad, angle_grad)


def solution(mesh):
    placed = (
        P("dp", "tensor"),
        P(None, "tensor"),
        P("dp", "tensor"),
        P("tensor", "dp"),
        P(),
        P("dp", "tensor"),
    )
    return jax.shard_map(
        body,
        mesh=mesh,
        in_specs=placed,
        out_specs=(P("dp", "tensor"), P(None, "tensor")),
        check_vma=False,
    )
```

profile of v0, /device:TPU:1, one launch (start us, length us, event | category | flops | bytes accessed | tf_op | source)
XLA Modules:
  0.0 559.8 jit_solution(14048898341933507902)
XLA Ops:
  9.9 24.0 %all_gather.9 = f32[14,8192]{1,0:T(8,128)S(1)} all-gather(f32[14,512]{1,0:T(8,128)} %param.9), channel_id=1, replica_groups=mesh['dp'=16,'tensor'=16] {'tensor'}, dimensions={1}, use_global_device_ids=true | all-gather | bytes 487424 | tf_op jit(solution)/shard_map/all_gather | solution.py:69
  34.3 6.2 %gather_fusion = f32[1024]{0:T(1024)S(1)} fusion(f32[8192]{0:T(1024)S(1)} %bitcast.62, s32[1024]{0:T(1024)S(1)} %get-tuple-element.213), kind=kCustom, calls=%fused_computation.clone | custom fusion | bytes 12288 | tf_op jit(solution)/shard_map/jit(_take)/gather | solution.py:45
  40.5 6.2 %gather_fusion.1 = f32[1024]{0:T(1024)S(1)} fusion(f32[8192]{0:T(1024)S(1)} %bitcast.61, s32[1024]{0:T(1024)S(1)} %get-tuple-element.226), kind=kCustom, calls=%fused_computation.1.clone | custom fusion | bytes 12288 | tf_op jit(solution)/shard_map/jit(_take)/gather | solution.py:45
  46.7 6.2 %gather_fusion.2 = f32[1024]{0:T(1024)S(1)} fusion(f32[8192]{0:T(1024)S(1)} %bitcast.60, s32[1024]{0:T(1024)S(1)} %get-tuple-element.214), kind=kCustom, calls=%fused_computation.2.clone | custom fusion | bytes 12288 | tf_op jit(solution)/shard_map/jit(_take)/gather | solution.py:45
  52.8 6.2 %gather_fusion.3 = f32[1024]{0:T(1024)S(1)} fusion(f32[8192]{0:T(1024)S(1)} %bitcast.59, s32[1024]{0:T(1024)S(1)} %get-tuple-element.215), kind=kCustom, calls=%fused_computation.3.clone | custom fusion | bytes 12288 | tf_op jit(solution)/shard_map/jit(_take)/gather | solution.py:45
  59.0 6.2 %gather_fusion.4 = f32[1024]{0:T(1024)S(1)} fusion(f32[8192]{0:T(1024)S(1)} %bitcast.58, s32[1024]{0:T(1024)S(1)} %get-tuple-element.216), kind=kCustom, calls=%fused_computation.4.clone | custom fusion | bytes 12288 | tf_op jit(solution)/shard_map/jit(_take)/gather | solution.py:45
  65.2 6.2 %gather_fusion.5 = f32[1024]{0:T(1024)S(1)} fusion(f32[8192]{0:T(1024)S(1)} %bitcast.57, s32[1024]{0:T(1024)S(1)} %get-tuple-element.217), kind=kCustom, calls=%fused_computation.5.clone | custom fusion | bytes 12288 | tf_op jit(solution)/shard_map/jit(_take)/gather | solution.py:45
  71.3 6.2 %gather_fusion.6 = f32[1024]{0:T(1024)S(1)} fusion(f32[8192]{0:T(1024)S(1)} %bitcast.56, s32[1024]{0:T(1024)S(1)} %get-tuple-element.218), kind=kCustom, calls=%fused_computation.6.clone | custom fusion | bytes 12288 | tf_op jit(solution)/shard_map/jit(_take)/gather | solution.py:45
  77.5 6.2 %gather_fusion.7 = f32[1024]{0:T(1024)S(1)} fusion(f32[8192]{0:T(1024)S(1)} %bitcast.55, s32[1024]{0:T(1024)S(1)} %get-tuple-element.219), kind=kCustom, calls=%fused_computation.7.clone | custom fusion | bytes 12288 | tf_op jit(solution)/shard_map/jit(_take)/gather | solution.py:45
  83.7 6.2 %gather_fusion.8 = f32[1024]{0:T(1024)S(1)} fusion(f32[8192]{0:T(1024)S(1)} %bitcast.54, s32[1024]{0:T(1024)S(1)} %get-tuple-element.220), kind=kCustom, calls=%fused_computation.8.clone | custom fusion | bytes 12288 | tf_op jit(solution)/shard_map/jit(_take)/gather | solution.py:45
  89.9 6.2 %gather_fusion.9 = f32[1024]{0:T(1024)S(1)} fusion(f32[8192]{0:T(1024)S(1)} %bitcast.53, s32[1024]{0:T(1024)S(1)} %get-tuple-element.221), kind=kCustom, calls=%fused_computation.9.clone | custom fusion | bytes 12288 | tf_op jit(solution)/shard_map/jit(_take)/gather | solution.py:45
  109.1 6.1 %gather_fusion.10 = f32[1024]{0:T(1024)S(1)} fusion(f32[8192]{0:T(1024)S(1)} %bitcast.52, s32[1024]{0:T(1024)S(1)} %get-tuple-element.222), kind=kCustom, calls=%fused_computation.10.clone | custom fusion | bytes 12288 | tf_op jit(solution)/shard_map/jit(_take)/gather | solution.py:45
  115.3 6.2 %gather_fusion.11 = f32[1024]{0:T(1024)S(1)} fusion(f32[8192]{0:T(1024)S(1)} %bitcast.51, s32[1024]{0:T(1024)S(1)} %get-tuple-element.223), kind=kCustom, calls=%fused_computation.11.clone | custom fusion | bytes 12288 | tf_op jit(solution)/shard_map/jit(_take)/gather | solution.py:45
  124.3 11.9 %collective-permute-done.5 = bf16[256,1024]{0,1:T(8,128)(2,1)S(1)} collective-permute-done((bf16[256,1024]{0,1:T(8,128)(2,1)}, bf16[256,1024]{0,1:T(8,128)(2,1)S(1)}, u32[]{:S(2)}, u32[]{:S(2)}) %collective-permute-start.5) | collective-permute-done | bytes 524320 | tf_op jit(solution)/shard_map/ppermute | solution.py:10
  137.7 58.5 %all-gather.3.cloned.1.call-done = bf16[1024,10240]{1,0:T(8,128)(2,1)} async-done(((bf16[1024,640]{1,0:T(8,128)(2,1)}), bf16[1024,10240]{1,0:T(8,128)(2,1)}) %all-gather.3.cloned.1.call-update) | async-done | bytes 20971536 | tf_op jit(solution)/shard_map/all_gather | solution.py:73
  196.2 12.5 %fusion.3 = f32[256,1024]{0,1:T(8,128)} fusion(bf16[256,10240]{1,0:T(8,128)(2,1)} %all-gather.5.cloned.1.call-done, bf16[1024,10240]{1,0:T(8,128)(2,1)} %all-gather.3.cloned.1.call-done, f32[10240]{0:T(1024)S(1)} %multiply_exponential_fusion, s32[256,1024]{0,1:T(8,128)} %copy.20, s32[256]{0:T(256)S(1)} %shift_right_arithmetic.224), kind=kOutput, calls=%fused_computation.32 | convolution fusion | flops 5401214976 | bytes 28353536 | tf_op jit(solution)/shard_map/dot_general | solution.py:75
  208.7 5.5 collective-permute-start
  214.2 6.1 %gather_fusion.12 = f32[1024]{0:T(1024)S(1)} fusion(f32[8192]{0:T(1024)S(1)} %bitcast.50, s32[1024]{0:T(1024)S(1)} %get-tuple-element.224), kind=kCustom, calls=%fused_computation.12.clone | custom fusion | bytes 12288 | tf_op jit(solution)/shard_map/jit(_take)/gather | solution.py:45
  220.4 2.2 fusion.57
  222.6 6.1 %gather_fusion.13 = f32[1024]{0:T(1024)S(1)} fusion(f32[8192]{0:T(1024)S(1)} %bitcast.49, s32[1024]{0:T(1024)S(1)} %get-tuple-element.225), kind=kCustom, calls=%fused_computation.13.clone | custom fusion | bytes 12288 | tf_op jit(solution)/shard_map/jit(_take)/gather | solution.py:45
  228.8 41.5 %collective-permute-done.7 = bf16[256,1024]{0,1:T(8,128)(2,1)} collective-permute-done((bf16[256,1024]{0,1:T(8,128)(2,1)}, bf16[256,1024]{0,1:T(8,128)(2,1)}, u32[]{:S(2)}, u32[]{:S(2)}) %collective-permute-start.7) | collective-permute-done | bytes 524320 | tf_op jit(solution)/shard_map/ppermute | solution.py:10
  270.3 2.7 multiply_reduce_fusion
  273.1 15.1 %collective-permute-start.1 = (f32[256,1024]{0,1:T(8,128)S(1)}, f32[256,1024]{0,1:T(8,128)S(1)}, u32[]{:S(2)}, u32[]{:S(2)}) collective-permute-start(f32[256,1024]{0,1:T(8,128)S(1)} %get-tuple-element.17), channel_id=1, source_target_pairs={{0,4},{1,5},{2,6},{3,7},{4,0},{5,1},{6,2},{7,3},{8,12},{9,13},{10,... | collective-permute-start | bytes 3145736 | tf_op jit(solution)/shard_map/ppermute | solution.py:10
  288.2 46.0 %collective-permute-done.1 = f32[256,1024]{0,1:T(8,128)S(1)} collective-permute-done((f32[256,1024]{0,1:T(8,128)S(1)}, f32[256,1024]{0,1:T(8,128)S(1)}, u32[]{:S(2)}, u32[]{:S(2)}) %collective-permute-start.1) | collective-permute-done | bytes 1048608 | tf_op jit(solution)/shard_map/ppermute | solution.py:10
  336.5 22.4 %collective-permute-done.2 = f32[256,1024]{0,1:T(8,128)S(1)} collective-permute-done((f32[256,1024]{0,1:T(8,128)S(1)}, f32[256,1024]{0,1:T(8,128)S(1)}, u32[]{:S(2)}, u32[]{:S(2)}) %collective-permute-start.2) | collective-permute-done | bytes 1048608 | tf_op jit(solution)/shard_map/ppermute | solution.py:10
  358.9 2.1 fusion.10
  364.9 7.7 %scatter_custom_fusion.13 = f32[8192]{0:T(1024)S(1)} fusion(s32[1024]{0:T(1024)S(1)} %bitcast.91, f32[1024]{0:T(1024)S(1)} %get-tuple-element.13, f32[]{:T(128)} %constant.42.clone.1), kind=kCustom, calls=%fused_computation.161 | custom fusion | flops 1024 | bytes 32772 | tf_op jit(solution)/shard_map/scatter-add | solution.py:59
  372.6 7.7 %scatter_custom_fusion.12 = f32[8192]{0:T(1024)S(1)} fusion(s32[1024]{0:T(1024)S(1)} %bitcast.89, f32[1024]{0:T(1024)S(1)} %get-tuple-element.14, f32[]{:T(128)} %constant.42.clone.1), kind=kCustom, calls=%fused_computation.163 | custom fusion | flops 1024 | bytes 32772 | tf_op jit(solution)/shard_map/scatter-add | solution.py:59
  380.3 7.7 %scatter_custom_fusion.11 = f32[8192]{0:T(1024)S(1)} fusion(s32[1024]{0:T(1024)S(1)} %bitcast.90, f32[1024]{0:T(1024)S(1)} %get-tuple-element.15, f32[]{:T(128)} %constant.42.clone.1), kind=kCustom, calls=%fused_computation.165 | custom fusion | flops 1024 | bytes 32772 | tf_op jit(solution)/shard_map/scatter-add | solution.py:59
  387.9 7.8 %scatter_custom_fusion.10 = f32[8192]{0:T(1024)S(1)} fusion(s32[1024]{0:T(1024)S(1)} %bitcast.88, f32[1024]{0:T(1024)S(1)} %get-tuple-element.16, f32[]{:T(128)} %constant.42.clone.1), kind=kCustom, calls=%fused_computation.167 | custom fusion | flops 1024 | bytes 32772 | tf_op jit(solution)/shard_map/scatter-add | solution.py:59
  395.8 2.4 multiply_reduce_fusion.1
  425.7 7.8 %scatter_custom_fusion.9 = f32[8192]{0:T(1024)S(1)} fusion(s32[1024]{0:T(1024)} %bitcast.79, f32[1024]{0:T(1024)S(1)} %get-tuple-element.23, f32[]{:T(128)} %constant.42.clone.1), kind=kCustom, calls=%fused_computation.169 | custom fusion | flops 1024 | bytes 33280 | tf_op jit(solution)/shard_map/scatter-add | solution.py:59
  433.5 7.8 %scatter_custom_fusion.8 = f32[8192]{0:T(1024)S(1)} fusion(s32[1024]{0:T(1024)} %bitcast.87, f32[1024]{0:T(1024)S(1)} %get-tuple-element.25, f32[]{:T(128)} %constant.42.clone.1), kind=kCustom, calls=%fused_computation.171 | custom fusion | flops 1024 | bytes 33280 | tf_op jit(solution)/shard_map/scatter-add | solution.py:59
  441.3 7.8 %scatter_custom_fusion.7 = f32[8192]{0:T(1024)S(1)} fusion(s32[1024]{0:T(1024)} %bitcast.86, f32[1024]{0:T(1024)S(1)} %get-tuple-element.27, f32[]{:T(128)} %constant.42.clone.1), kind=kCustom, calls=%fused_computation.173 | custom fusion | flops 1024 | bytes 33280 | tf_op jit(solution)/shard_map/scatter-add | solution.py:59
  449.1 7.8 %scatter_custom_fusion.6 = f32[8192]{0:T(1024)S(1)} fusion(s32[1024]{0:T(1024)} %bitcast.81, f32[1024]{0:T(1024)S(1)} %get-tuple-element.29, f32[]{:T(128)} %constant.42.clone.1), kind=kCustom, calls=%fused_computation.175 | custom fusion | flops 1024 | bytes 33280 | tf_op jit(solution)/shard_map/scatter-add | solution.py:59
  456.9 7.8 %scatter_custom_fusion.5 = f32[8192]{0:T(1024)S(1)} fusion(s32[1024]{0:T(1024)} %bitcast.80, f32[1024]{0:T(1024)S(1)} %get-tuple-element.31, f32[]{:T(128)} %constant.42.clone.1), kind=kCustom, calls=%fused_computation.177 | custom fusion | flops 1024 | bytes 33280 | tf_op jit(solution)/shard_map/scatter-add | solution.py:59
  464.7 7.8 %scatter_custom_fusion.4 = f32[8192]{0:T(1024)S(1)} fusion(s32[1024]{0:T(1024)} %bitcast.83, f32[1024]{0:T(1024)S(1)} %get-tuple-element.33, f32[]{:T(128)} %constant.42.clone.1), kind=kCustom, calls=%fused_computation.179 | custom fusion | flops 1024 | bytes 33280 | tf_op jit(solution)/shard_map/scatter-add | solution.py:59
  472.5 7.8 %scatter_custom_fusion.3 = f32[8192]{0:T(1024)S(1)} fusion(s32[1024]{0:T(1024)} %bitcast.82, f32[1024]{0:T(1024)S(1)} %get-tuple-element.35, f32[]{:T(128)} %constant.42.clone.1), kind=kCustom, calls=%fused_computation.181 | custom fusion | flops 1024 | bytes 33280 | tf_op jit(solution)/shard_map/scatter-add | solution.py:59
  480.3 7.8 %scatter_custom_fusion.2 = f32[8192]{0:T(1024)S(1)} fusion(s32[1024]{0:T(1024)} %bitcast.85, f32[1024]{0:T(1024)S(1)} %get-tuple-element.37, f32[]{:T(128)} %constant.42.clone.1), kind=kCustom, calls=%fused_computation.183 | custom fusion | flops 1024 | bytes 33280 | tf_op jit(solution)/shard_map/scatter-add | solution.py:59
  488.1 8.6 %scatter_custom_fusion.1 = f32[8192]{0:T(1024)} fusion(s32[1024]{0:T(1024)} %bitcast.84, f32[1024]{0:T(1024)S(1)} %get-tuple-element.39, f32[]{:T(128)} %constant.42.clone.1), kind=kCustom, calls=%fused_computation.185 | custom fusion | flops 1024 | bytes 33280 | tf_op jit(solution)/shard_map/scatter-add | solution.py:59
  496.7 3.8 fusion.56
  500.5 7.8 %scatter_custom_fusion = f32[8192]{0:T(1024)S(1)} fusion(s32[1024]{0:T(1024)} %bitcast.78, f32[1024]{0:T(1024)} %get-tuple-element.41, f32[]{:T(128)} %constant.42.clone.1), kind=kCustom, calls=%fused_computation.187 | custom fusion | flops 1024 | bytes 33280 | tf_op jit(solution)/shard_map/scatter-add | solution.py:59
  508.3 2.8 stack.59
  511.1 4.1 all-to-all-start
  515.4 17.1 %all-to-all-done = f32[16,14,512]{2,1,0:T(8,128)} async-done(((f32[16,14,512]{2,1,0:T(8,128)}), f32[16,14,512]{2,1,0:T(8,128)}, u32[]{:S(2)}, u32[]{:S(2)}) %all-to-all-start) | async-done | bytes 458784 | tf_op jit(solution)/shard_map/all_to_all | solution.py:21
  534.5 5.0 all-to-all-start.1
  539.5 2.7 fusion.35
  544.2 6.6 %all-to-all-done.1 = f32[16,14,512]{2,1,0:T(8,128)} async-done(((f32[16,14,512]{2,1,0:T(8,128)}), f32[16,14,512]{2,1,0:T(8,128)}, u32[]{:S(2)}, u32[]{:S(2)}) %all-to-all-start.1) | async-done | bytes 458784 | tf_op jit(solution)/shard_map/all_to_all | solution.py:27
  (161 shorter events, 59.6 us)
Async XLA Ops:
  7.2 130.6 %all-gather.5.cloned.1.call-start = ((), (), s32[]{:S(2)}) async-start(), calls=%async_computation.3 | async-start | bytes 5570560 | tf_op jit(solution)/shard_map/all_gather | solution.py:71
  7.9 188.3 %all-gather.3.cloned.1.call-start = ((), (), s32[]{:S(2)}) async-start(), calls=%async_computation.2 | async-start | bytes 22282240 | tf_op jit(solution)/shard_map/all_gather | solution.py:73
  96.0 7.1 %copy-start.3 = (pred[1024]{0:T(1024)(128)(4,1)}, pred[1024]{0:T(1024)(128)(4,1)S(1)}, u32[]{:S(2)}) copy-start(pred[1024]{0:T(1024)(128)(4,1)S(1)} %and_compare_fusion) | copy-start | bytes 3076
  96.1 325.9 %copy-start.2 = (pred[1024]{0:T(1024)(128)(4,1)}, pred[1024]{0:T(1024)(128)(4,1)S(1)}, u32[]{:S(2)}) copy-start(pred[1024]{0:T(1024)(128)(4,1)S(1)} %get-tuple-element.245) | copy-start | bytes 3076
  104.2 18.6 %copy-start = (s32[16,1024]{1,0:T(8,128)S(1)}, s32[16,1024]{1,0:T(8,128)}, u32[]{:S(2)}) copy-start(s32[16,1024]{1,0:T(8,128)} %param.10) | copy-start | bytes 196612
  104.4 19.9 %copy-start.1 = (s32[10240]{0:T(1024)S(1)}, s32[10240]{0:T(1024)}, u32[]{:S(2)}) copy-start(s32[10240]{0:T(1024)} %param.12) | copy-start | bytes 122884
  108.6 13.0 %collective-permute-start.4 = (bf16[256,1024]{0,1:T(8,128)(2,1)S(1)}, bf16[256,1024]{0,1:T(8,128)(2,1)S(1)}, u32[]{:S(2)}, u32[]{:S(2)}) collective-permute-start(bf16[256,1024]{0,1:T(8,128)(2,1)S(1)} %get-tuple-element.21), channel_id=1, source_target_pairs={{0,1},{1,0},{2,3},{3,2},{4,5},{5,4},{6,7},{7,6},{8,9},{9,8},{10,11... | collective-permute-start | bytes 1572872 | tf_op jit(solution)/shard_map/ppermute | solution.py:10
  122.7 13.5 %collective-permute-start.5 = (bf16[256,1024]{0,1:T(8,128)(2,1)}, bf16[256,1024]{0,1:T(8,128)(2,1)S(1)}, u32[]{:S(2)}, u32[]{:S(2)}) collective-permute-start(bf16[256,1024]{0,1:T(8,128)(2,1)} %fusion.182), channel_id=1, source_target_pairs={{0,2},{1,3},{2,0},{3,1},{4,6},{5,7},{6,4},{7,5},{8,10},{9,11},{10,... | collective-permute-start | bytes 1572872 | tf_op jit(solution)/shard_map/ppermute | solution.py:10
  137.7 82.7 %collective-permute-start.6 = (bf16[256,1024]{0,1:T(8,128)(2,1)}, bf16[256,1024]{0,1:T(8,128)(2,1)}, u32[]{:S(2)}, u32[]{:S(2)}) collective-permute-start(bf16[256,1024]{0,1:T(8,128)(2,1)} %get-tuple-element.18), channel_id=1, source_target_pairs={{0,4},{1,5},{2,6},{3,7},{4,0},{5,1},{6,2},{7,3},{8,12},{9,13},{10,... | collective-permute-start | bytes 1572872 | tf_op jit(solution)/shard_map/ppermute | solution.py:10
  208.7 61.6 %collective-permute-start = (f32[256,1024]{0,1:T(8,128)}, f32[256,1024]{0,1:T(8,128)}, u32[]{:S(2)}, u32[]{:S(2)}) collective-permute-start(f32[256,1024]{0,1:T(8,128)} %fusion.3), channel_id=1, source_target_pairs={{0,8},{1,9},{2,10},{3,11},{4,12},{5,13},{6,14},{7,15},{8,0},{9,1},... | collective-permute-start | bytes 3145736 | tf_op jit(solution)/shard_map/ppermute | solution.py:10
  222.6 47.7 %collective-permute-start.7 = (bf16[256,1024]{0,1:T(8,128)(2,1)}, bf16[256,1024]{0,1:T(8,128)(2,1)}, u32[]{:S(2)}, u32[]{:S(2)}) collective-permute-start(bf16[256,1024]{0,1:T(8,128)(2,1)} %fusion.57), channel_id=1, source_target_pairs={{0,8},{1,9},{2,10},{3,11},{4,12},{5,13},{6,14},{7,15},{8,0},{9,1},... | collective-permute-start | bytes 1572872 | tf_op jit(solution)/shard_map/ppermute | solution.py:10
  273.1 61.2 %collective-permute-start.1 = (f32[256,1024]{0,1:T(8,128)S(1)}, f32[256,1024]{0,1:T(8,128)S(1)}, u32[]{:S(2)}, u32[]{:S(2)}) collective-permute-start(f32[256,1024]{0,1:T(8,128)S(1)} %get-tuple-element.17), channel_id=1, source_target_pairs={{0,4},{1,5},{2,6},{3,7},{4,0},{5,1},{6,2},{7,3},{8,12},{9,13},{10,... | collective-permute-start | bytes 3145736 | tf_op jit(solution)/shard_map/ppermute | solution.py:10
  334.6 24.3 %collective-permute-start.2 = (f32[256,1024]{0,1:T(8,128)S(1)}, f32[256,1024]{0,1:T(8,128)S(1)}, u32[]{:S(2)}, u32[]{:S(2)}) collective-permute-start(f32[256,1024]{0,1:T(8,128)S(1)} %multiply_subtract_fusion.11), channel_id=1, source_target_pairs={{0,2},{1,3},{2,0},{3,1},{4,6},{5,7},{6,4},{7,5},{8,10},{9,11},{10,... | collective-permute-start | bytes 3145736 | tf_op jit(solution)/shard_map/ppermute | solution.py:10
  361.0 34.8 %collective-permute-start.3 = (f32[256,1024]{0,1:T(8,128)}, f32[256,1024]{0,1:T(8,128)S(1)}, u32[]{:S(2)}, u32[]{:S(2)}) collective-permute-start(f32[256,1024]{0,1:T(8,128)} %get-tuple-element.20), channel_id=1, source_target_pairs={{0,1},{1,0},{2,3},{3,2},{4,5},{5,4},{6,7},{7,6},{8,9},{9,8},{10,11... | collective-permute-start | bytes 3145736 | tf_op jit(solution)/shard_map/ppermute | solution.py:10
  511.1 21.4 %all-to-all-start = ((f32[16,14,512]{2,1,0:T(8,128)}), f32[16,14,512]{2,1,0:T(8,128)}, u32[]{:S(2)}, u32[]{:S(2)}) async-start(f32[16,14,512]{2,1,0:T(8,128)} %bitcast.44), calls=%async_computation | async-start | bytes 1048576 | tf_op jit(solution)/shard_map/all_to_all | solution.py:21
  534.5 16.4 %all-to-all-start.1 = ((f32[16,14,512]{2,1,0:T(8,128)}), f32[16,14,512]{2,1,0:T(8,128)}, u32[]{:S(2)}, u32[]{:S(2)}) async-start(f32[16,14,512]{2,1,0:T(8,128)} %broadcast_in_dim.368), calls=%async_computation.1 | async-start | bytes 1048576 | tf_op jit(solution)/shard_map/all_to_all | solution.py:27
Sparse Core Ops, SparseCore 0:
  9.8 48.4 all-gather.4
  60.7 135.4 all-gather.2
where the time goes:
time: 569 us; the launch traced here: 560 us
  waiting for transfers between devices  205 us (36%)
  other arithmetic  167 us (29%)
  local copies, waits for them, and re-layouts  103 us (18%)
  starting transfers between devices  31.8 us (6%)
  blocking collectives  24 us (4%)
  between operations  15.6 us (3%)
  matrix products  12.5 us (2%)
    ppermute x8, waiting for transfers between devices, partner(): return lax.ppermute(value, axis, pairs)  122 us
    scatter-add x14, other arithmetic, scatter_terms(): return jnp.zeros((half_pairs,), jnp.float32).at[pair].add(term)  110 us
    gather x14, local copies, waits for them, and re-layouts, section_terms(): theta = jnp.take(table[section], pair)  86.1 us
    all_gather x1, waiting for transfers between devices, body(): lax.all_gather(codes, 'dp', axis=1, tiled=True).astype(jnp.float32)  58.5 us
    all_gather x1, blocking collectives, body(): table = lax.all_gather(angles, 'tensor', axis=1, tiled=True)  24 us
    reduce_sum x12, other arithmetic, body(): jnp.sum(sign * grad * other, axis=0)  23.8 us
    ppermute x8, starting transfers between devices, partner(): return lax.ppermute(value, axis, pairs)  22.6 us
    all_to_all x1, waiting for transfers between devices, sent_and_summed(): parts = lax.all_to_all(split_up(value, dim, count), axis, 0, 0, tiled=True)  17.1 us
  transfers between devices with their start and end apart: 12, of which 7 were waited for; matrix products, arithmetic and copies ran while one was open for 28% of the time, Pallas kernels for 0%

commit v1 on v0

--- a/solution.py
+++ b/solution.py
@@ -66,7 +66,14 @@
     half_pairs = share * lax.axis_size("tensor")
     local_count = width.bit_length() - 1
     place = lax.axis_index("tensor")
-    table = lax.all_gather(angles, "tensor", axis=1, tiled=True)
+    ring = [angles]
+    for hop in range(15):
+        ring.append(lax.ppermute(ring[-1], "tensor", [(dev, (dev + 1) % 16) for dev in range(16)]))
+    table = jnp.roll(
+        jnp.concatenate(ring[::-1], axis=1),
+        (lax.axis_index("tensor") + 1) * ring[0].shape[1],
+        axis=1,
+    )
     scale = jnp.exp2(exponents.astype(jnp.float32))
     full_cot = lax.all_gather(cotangent, "tensor", axis=1, tiled=True)
     weight_piece = (

time: 569 us -> 562 us (0.988)
  blocking collectives: 24 us -> 0 us
  waiting for transfers between devices: 205 us -> 219 us
  starting transfers between devices: 31.8 us -> 41.3 us
    ppermute x0 -> x15, waiting for transfers between devices: none -> 62.9 us  [body(): lax.ppermute(ring[-1], 'tensor', [(dev, (dev + 1) % 16) for dev in range(...]
    all_gather x1, waiting for transfers between devices: 58.5 us -> 12.3 us  [body(): lax.all_gather(codes, 'dp', axis=1, tiled=True).astype(jnp.float32)]
    all_gather x1 -> x0, blocking collectives: 24 us -> none  [body(): table = lax.all_gather(angles, 'tensor', axis=1, tiled=True)]
    ppermute x0 -> x15, starting transfers between devices: none -> 5.89 us  [body(): lax.ppermute(ring[-1], 'tensor', [(dev, (dev + 1) % 16) for dev in range(...]
  transfers between devices with their start and end apart: 12 -> 27, of which waited for: 7 -> 22; matrix products, arithmetic and copies ran while one was open for 28% -> 29% of each run, Pallas kernels for 0% -> 0%
where the time goes in v1:
time: 562 us; the launch traced here: 558 us
  waiting for transfers between devices  219 us (39%)
  other arithmetic  164 us (29%)
  local copies, waits for them, and re-layouts  106 us (19%)
  starting transfers between devices  41.3 us (7%)
  between operations  15.9 us (3%)
  matrix products  12.5 us (2%)
    ppermute x8, waiting for transfers between devices, partner(): return lax.ppermute(value, axis, pairs)  118 us
    scatter-add x14, other arithmetic, scatter_terms(): return jnp.zeros((half_pairs,), jnp.float32).at[pair].add(term)  108 us
    gather x14, local copies, waits for them, and re-layouts, section_terms(): theta = jnp.take(table[section], pair)  86.7 us
    ppermute x15, waiting for transfers between devices, body(): lax.ppermute(ring[-1], 'tensor', [(dev, (dev + 1) % 16) for dev in range(...  62.9 us
    ppermute x8, starting transfers between devices, partner(): return lax.ppermute(value, axis, pairs)  26.2 us
    reduce_sum x12, other arithmetic, body(): jnp.sum(sign * grad * other, axis=0)  24.1 us
    all_to_all x1, waiting for transfers between devices, sent_and_summed(): parts = lax.all_to_all(split_up(value, dim, count), axis, 0, 0, tiled=True)  17.1 us
    dot_general x1, matrix products, body(): lax.dot_general(full_cot, weight_piece, (((1,), (1,)), ((), ())), preferr...  12.5 us
  transfers between devices with their start and end apart: 27, of which 22 were waited for; matrix products, arithmetic and copies ran while one was open for 29% of the time, Pallas kernels for 0%

profile of v1, /device:TPU:1, one launch (start us, length us, event | category | flops | bytes accessed | tf_op | source)
XLA Modules:
  0.0 558.4 jit_solution(839142587188800612)
XLA Ops:
  22.5 4.5 collective-permute-done.3
  27.1 5.0 collective-permute-done.4
  32.1 5.0 collective-permute-done.5
  37.1 4.9 collective-permute-done.6
  42.0 4.9 collective-permute-done.7
  47.5 4.6 collective-permute-done.8
  52.1 4.8 collective-permute-done.9
  56.9 4.5 collective-permute-done.10
  66.0 4.5 collective-permute-done.12
  82.5 6.3 %gather_fusion = f32[1024]{0:T(1024)S(1)} fusion(f32[8192]{0:T(1024)S(1)} %bitcast.62, s32[1024]{0:T(1024)S(1)} %get-tuple-element.213), kind=kCustom, calls=%fused_computation.clone | custom fusion | bytes 12288 | tf_op jit(solution)/shard_map/jit(_take)/gather | solution.py:45
  88.8 6.2 %gather_fusion.1 = f32[1024]{0:T(1024)S(1)} fusion(f32[8192]{0:T(1024)S(1)} %bitcast.61, s32[1024]{0:T(1024)S(1)} %get-tuple-element.226), kind=kCustom, calls=%fused_computation.1.clone | custom fusion | bytes 12288 | tf_op jit(solution)/shard_map/jit(_take)/gather | solution.py:45
  95.0 6.2 %gather_fusion.2 = f32[1024]{0:T(1024)S(1)} fusion(f32[8192]{0:T(1024)S(1)} %bitcast.60, s32[1024]{0:T(1024)S(1)} %get-tuple-element.214), kind=kCustom, calls=%fused_computation.2.clone | custom fusion | bytes 12288 | tf_op jit(solution)/shard_map/jit(_take)/gather | solution.py:45
  101.1 6.2 %gather_fusion.3 = f32[1024]{0:T(1024)S(1)} fusion(f32[8192]{0:T(1024)S(1)} %bitcast.59, s32[1024]{0:T(1024)S(1)} %get-tuple-element.215), kind=kCustom, calls=%fused_computation.3.clone | custom fusion | bytes 12288 | tf_op jit(solution)/shard_map/jit(_take)/gather | solution.py:45
  107.3 6.2 %gather_fusion.4 = f32[1024]{0:T(1024)S(1)} fusion(f32[8192]{0:T(1024)S(1)} %bitcast.58, s32[1024]{0:T(1024)S(1)} %get-tuple-element.216), kind=kCustom, calls=%fused_computation.4.clone | custom fusion | bytes 12288 | tf_op jit(solution)/shard_map/jit(_take)/gather | solution.py:45
  113.4 6.2 %gather_fusion.5 = f32[1024]{0:T(1024)S(1)} fusion(f32[8192]{0:T(1024)S(1)} %bitcast.57, s32[1024]{0:T(1024)S(1)} %get-tuple-element.217), kind=kCustom, calls=%fused_computation.5.clone | custom fusion | bytes 12288 | tf_op jit(solution)/shard_map/jit(_take)/gather | solution.py:45
  119.6 6.2 %gather_fusion.6 = f32[1024]{0:T(1024)S(1)} fusion(f32[8192]{0:T(1024)S(1)} %bitcast.56, s32[1024]{0:T(1024)S(1)} %get-tuple-element.218), kind=kCustom, calls=%fused_computation.6.clone | custom fusion | bytes 12288 | tf_op jit(solution)/shard_map/jit(_take)/gather | solution.py:45
  125.8 6.2 %gather_fusion.7 = f32[1024]{0:T(1024)S(1)} fusion(f32[8192]{0:T(1024)S(1)} %bitcast.55, s32[1024]{0:T(1024)S(1)} %get-tuple-element.219), kind=kCustom, calls=%fused_computation.7.clone | custom fusion | bytes 12288 | tf_op jit(solution)/shard_map/jit(_take)/gather | solution.py:45
  131.9 6.2 %gather_fusion.8 = f32[1024]{0:T(1024)S(1)} fusion(f32[8192]{0:T(1024)S(1)} %bitcast.54, s32[1024]{0:T(1024)S(1)} %get-tuple-element.220), kind=kCustom, calls=%fused_computation.8.clone | custom fusion | bytes 12288 | tf_op jit(solution)/shard_map/jit(_take)/gather | solution.py:45
  138.1 6.2 %gather_fusion.9 = f32[1024]{0:T(1024)S(1)} fusion(f32[8192]{0:T(1024)S(1)} %bitcast.53, s32[1024]{0:T(1024)S(1)} %get-tuple-element.221), kind=kCustom, calls=%fused_computation.9.clone | custom fusion | bytes 12288 | tf_op jit(solution)/shard_map/jit(_take)/gather | solution.py:45
  162.1 6.6 %gather_fusion.10 = f32[1024]{0:T(1024)S(1)} fusion(f32[8192]{0:T(1024)S(1)} %bitcast.52, s32[1024]{0:T(1024)S(1)} %get-tuple-element.222), kind=kCustom, calls=%fused_computation.10.clone | custom fusion | bytes 12288 | tf_op jit(solution)/shard_map/jit(_take)/gather | solution.py:45
  169.2 6.2 %gather_fusion.11 = f32[1024]{0:T(1024)S(1)} fusion(f32[8192]{0:T(1024)S(1)} %bitcast.51, s32[1024]{0:T(1024)S(1)} %get-tuple-element.223), kind=kCustom, calls=%fused_computation.11.clone | custom fusion | bytes 12288 | tf_op jit(solution)/shard_map/jit(_take)/gather | solution.py:45
  175.4 7.4 %collective-permute-done.20 = bf16[256,1024]{0,1:T(8,128)(2,1)S(1)} collective-permute-done((bf16[256,1024]{0,1:T(8,128)(2,1)S(1)}, bf16[256,1024]{0,1:T(8,128)(2,1)S(1)}, u32[]{:S(2)}, u32[]{:S(2)}) %collective-permute-start.20) | collective-permute-done | bytes 524320 | tf_op jit(solution)/shard_map/ppermute | solution.py:10
  184.5 12.3 %all-gather.3.cloned.1.call-done = bf16[1024,10240]{1,0:T(8,128)(2,1)} async-done(((bf16[1024,640]{1,0:T(8,128)(2,1)}), bf16[1024,10240]{1,0:T(8,128)(2,1)}) %all-gather.3.cloned.1.call-update) | async-done | bytes 20971536 | tf_op jit(solution)/shard_map/all_gather | solution.py:80
  196.9 12.5 %fusion.3 = f32[256,1024]{0,1:T(8,128)} fusion(bf16[256,10240]{1,0:T(8,128)(2,1)} %all-gather.5.cloned.1.call-done, bf16[1024,10240]{1,0:T(8,128)(2,1)} %all-gather.3.cloned.1.call-done, f32[10240]{0:T(1024)S(1)} %multiply_exponential_fusion, s32[256,1024]{0,1:T(8,128)} %copy.20, s32[256]{0:T(256)S(1)} %shift_right_arithmetic.224), kind=kOutput, calls=%fused_computation.32 | convolution fusion | flops 5401214976 | bytes 28353536 | tf_op jit(solution)/shard_map/dot_general | solution.py:82
  209.4 5.4 collective-permute-start.15
  214.8 6.1 %gather_fusion.12 = f32[1024]{0:T(1024)S(1)} fusion(f32[8192]{0:T(1024)S(1)} %bitcast.50, s32[1024]{0:T(1024)S(1)} %get-tuple-element.224), kind=kCustom, calls=%fused_computation.12.clone | custom fusion | bytes 12288 | tf_op jit(solution)/shard_map/jit(_take)/gather | solution.py:45
  223.2 6.2 %gather_fusion.13 = f32[1024]{0:T(1024)S(1)} fusion(f32[8192]{0:T(1024)S(1)} %bitcast.49, s32[1024]{0:T(1024)S(1)} %copy-done.18), kind=kCustom, calls=%fused_computation.13.clone | custom fusion | bytes 12288 | tf_op jit(solution)/shard_map/jit(_take)/gather | solution.py:45
  229.4 41.5 %collective-permute-done.22 = bf16[256,1024]{0,1:T(8,128)(2,1)} collective-permute-done((bf16[256,1024]{0,1:T(8,128)(2,1)}, bf16[256,1024]{0,1:T(8,128)(2,1)}, u32[]{:S(2)}, u32[]{:S(2)}) %collective-permute-start.22) | collective-permute-done | bytes 524320 | tf_op jit(solution)/shard_map/ppermute | solution.py:10
  273.7 15.1 %collective-permute-start.16 = (f32[256,1024]{0,1:T(8,128)S(1)}, f32[256,1024]{0,1:T(8,128)S(1)}, u32[]{:S(2)}, u32[]{:S(2)}) collective-permute-start(f32[256,1024]{0,1:T(8,128)S(1)} %get-tuple-element.17), channel_id=1, source_target_pairs={{0,4},{1,5},{2,6},{3,7},{4,0},{5,1},{6,2},{7,3},{8,12},{9,13},{10,... | collective-permute-start | bytes 3145736 | tf_op jit(solution)/shard_map/ppermute | solution.py:10
  288.8 46.1 %collective-permute-done.16 = f32[256,1024]{0,1:T(8,128)S(1)} collective-permute-done((f32[256,1024]{0,1:T(8,128)S(1)}, f32[256,1024]{0,1:T(8,128)S(1)}, u32[]{:S(2)}, u32[]{:S(2)}) %collective-permute-start.16) | collective-permute-done | bytes 1048608 | tf_op jit(solution)/shard_map/ppermute | solution.py:10
  336.0 23.5 %collective-permute-done.17 = f32[256,1024]{0,1:T(8,128)S(1)} collective-permute-done((f32[256,1024]{0,1:T(8,128)S(1)}, f32[256,1024]{0,1:T(8,128)S(1)}, u32[]{:S(2)}, u32[]{:S(2)}) %collective-permute-start.17) | collective-permute-done | bytes 1048608 | tf_op jit(solution)/shard_map/ppermute | solution.py:10
  364.4 7.7 %scatter_custom_fusion.13 = f32[8192]{0:T(1024)S(1)} fusion(s32[1024]{0:T(1024)S(1)} %bitcast.91, f32[1024]{0:T(1024)S(1)} %get-tuple-element.13, f32[]{:T(128)} %constant.115.clone.1), kind=kCustom, calls=%fused_computation.193 | custom fusion | flops 1024 | bytes 32772 | tf_op jit(solution)/shard_map/scatter-add | solution.py:59
  372.1 7.7 %scatter_custom_fusion.12 = f32[8192]{0:T(1024)S(1)} fusion(s32[1024]{0:T(1024)S(1)} %bitcast.89, f32[1024]{0:T(1024)S(1)} %get-tuple-element.14, f32[]{:T(128)} %constant.115.clone.1), kind=kCustom, calls=%fused_computation.195 | custom fusion | flops 1024 | bytes 32772 | tf_op jit(solution)/shard_map/scatter-add | solution.py:59
  379.7 7.7 %scatter_custom_fusion.11 = f32[8192]{0:T(1024)S(1)} fusion(s32[1024]{0:T(1024)S(1)} %bitcast.90, f32[1024]{0:T(1024)S(1)} %get-tuple-element.15, f32[]{:T(128)} %constant.115.clone.1), kind=kCustom, calls=%fused_computation.197 | custom fusion | flops 1024 | bytes 32772 | tf_op jit(solution)/shard_map/scatter-add | solution.py:59
  387.4 7.7 %scatter_custom_fusion.10 = f32[8192]{0:T(1024)S(1)} fusion(s32[1024]{0:T(1024)S(1)} %bitcast.88, f32[1024]{0:T(1024)S(1)} %get-tuple-element.16, f32[]{:T(128)} %constant.115.clone.1), kind=kCustom, calls=%fused_computation.199 | custom fusion | flops 1024 | bytes 32772 | tf_op jit(solution)/shard_map/scatter-add | solution.py:59
  425.4 7.7 %scatter_custom_fusion.9 = f32[8192]{0:T(1024)S(1)} fusion(s32[1024]{0:T(1024)S(1)} %bitcast.79, f32[1024]{0:T(1024)S(1)} %get-tuple-element.23, f32[]{:T(128)} %constant.115.clone.1), kind=kCustom, calls=%fused_computation.201 | custom fusion | flops 1024 | bytes 32772 | tf_op jit(solution)/shard_map/scatter-add | solution.py:59
  433.1 7.7 %scatter_custom_fusion.8 = f32[8192]{0:T(1024)S(1)} fusion(s32[1024]{0:T(1024)S(1)} %bitcast.87, f32[1024]{0:T(1024)S(1)} %get-tuple-element.25, f32[]{:T(128)} %constant.115.clone.1), kind=kCustom, calls=%fused_computation.203 | custom fusion | flops 1024 | bytes 32772 | tf_op jit(solution)/shard_map/scatter-add | solution.py:59
  440.7 7.7 %scatter_custom_fusion.7 = f32[8192]{0:T(1024)S(1)} fusion(s32[1024]{0:T(1024)S(1)} %bitcast.86, f32[1024]{0:T(1024)S(1)} %get-tuple-element.27, f32[]{:T(128)} %constant.115.clone.1), kind=kCustom, calls=%fused_computation.205 | custom fusion | flops 1024 | bytes 32772 | tf_op jit(solution)/shard_map/scatter-add | solution.py:59
  448.4 7.7 %scatter_custom_fusion.6 = f32[8192]{0:T(1024)S(1)} fusion(s32[1024]{0:T(1024)S(1)} %bitcast.81, f32[1024]{0:T(1024)S(1)} %get-tuple-element.29, f32[]{:T(128)} %constant.115.clone.1), kind=kCustom, calls=%fused_computation.207 | custom fusion | flops 1024 | bytes 32772 | tf_op jit(solution)/shard_map/scatter-add | solution.py:59
  456.1 7.7 %scatter_custom_fusion.5 = f32[8192]{0:T(1024)S(1)} fusion(s32[1024]{0:T(1024)S(1)} %bitcast.80, f32[1024]{0:T(1024)S(1)} %get-tuple-element.31, f32[]{:T(128)} %constant.115.clone.1), kind=kCustom, calls=%fused_computation.209 | custom fusion | flops 1024 | bytes 32772 | tf_op jit(solution)/shard_map/scatter-add | solution.py:59
  463.7 7.7 %scatter_custom_fusion.4 = f32[8192]{0:T(1024)S(1)} fusion(s32[1024]{0:T(1024)S(1)} %bitcast.83, f32[1024]{0:T(1024)S(1)} %get-tuple-element.33, f32[]{:T(128)} %constant.115.clone.1), kind=kCustom, calls=%fused_computation.211 | custom fusion | flops 1024 | bytes 32772 | tf_op jit(solution)/shard_map/scatter-add | solution.py:59
  471.4 7.7 %scatter_custom_fusion.3 = f32[8192]{0:T(1024)S(1)} fusion(s32[1024]{0:T(1024)S(1)} %bitcast.82, f32[1024]{0:T(1024)S(1)} %get-tuple-element.35, f32[]{:T(128)} %constant.115.clone.1), kind=kCustom, calls=%fused_computation.213 | custom fusion | flops 1024 | bytes 32772 | tf_op jit(solution)/shard_map/scatter-add | solution.py:59
  479.1 7.8 %scatter_custom_fusion.2 = f32[8192]{0:T(1024)S(1)} fusion(s32[1024]{0:T(1024)} %bitcast.85, f32[1024]{0:T(1024)S(1)} %get-tuple-element.37, f32[]{:T(128)} %constant.115.clone.1), kind=kCustom, calls=%fused_computation.215 | custom fusion | flops 1024 | bytes 33280 | tf_op jit(solution)/shard_map/scatter-add | solution.py:59
  486.9 8.6 %scatter_custom_fusion.1 = f32[8192]{0:T(1024)} fusion(s32[1024]{0:T(1024)} %bitcast.84, f32[1024]{0:T(1024)S(1)} %get-tuple-element.39, f32[]{:T(128)} %constant.115.clone.1), kind=kCustom, calls=%fused_computation.217 | custom fusion | flops 1024 | bytes 33280 | tf_op jit(solution)/shard_map/scatter-add | solution.py:59
  499.3 7.8 %scatter_custom_fusion = f32[8192]{0:T(1024)S(1)} fusion(s32[1024]{0:T(1024)} %bitcast.78, f32[1024]{0:T(1024)} %get-tuple-element.41, f32[]{:T(128)} %constant.115.clone.1), kind=kCustom, calls=%fused_computation.219 | custom fusion | flops 1024 | bytes 33280 | tf_op jit(solution)/shard_map/scatter-add | solution.py:59
  514.2 17.1 %all-to-all-done = f32[16,14,512]{2,1,0:T(8,128)} async-done(((f32[16,14,512]{2,1,0:T(8,128)}), f32[16,14,512]{2,1,0:T(8,128)}, u32[]{:S(2)}, u32[]{:S(2)}) %all-to-all-start) | async-done | bytes 458784 | tf_op jit(solution)/shard_map/all_to_all | solution.py:21
  533.3 5.0 all-to-all-start.1
  543.0 6.7 %all-to-all-done.1 = f32[16,14,512]{2,1,0:T(8,128)} async-done(((f32[16,14,512]{2,1,0:T(8,128)}), f32[16,14,512]{2,1,0:T(8,128)}, u32[]{:S(2)}, u32[]{:S(2)}) %all-to-all-start.1) | async-done | bytes 458784 | tf_op jit(solution)/shard_map/all_to_all | solution.py:27
  (254 shorter events, 112.0 us)
Async XLA Ops:
  7.2 177.3 %all-gather.5.cloned.1.call-start = ((), (), s32[]{:S(2)}) async-start(), calls=%async_computation.3 | async-start | bytes 5570560 | tf_op jit(solution)/shard_map/all_gather | solution.py:78
  7.9 189.0 %all-gather.3.cloned.1.call-start = ((), (), s32[]{:S(2)}) async-start(), calls=%async_computation.2 | async-start | bytes 22282240 | tf_op jit(solution)/shard_map/all_gather | solution.py:80
  8.6 4.4 collective-permute-start
  13.0 4.9 collective-permute-start.1
  18.0 4.6 collective-permute-start.2
  22.5 4.6 collective-permute-start.3
  27.1 5.1 collective-permute-start.4
  32.1 5.0 collective-permute-start.5
  37.1 4.9 collective-permute-start.6
  42.0 4.9 collective-permute-start.7
  46.9 5.2 collective-permute-start.8
  52.1 4.8 collective-permute-start.9
  56.9 4.6 collective-permute-start.10
  56.9 96.8 %copy-start.12 = (pred[1024]{0:T(1024)(128)(4,1)}, pred[1024]{0:T(1024)(128)(4,1)S(1)}, u32[]{:S(2)}) copy-start(pred[1024]{0:T(1024)(128)(4,1)S(1)} %get-tuple-element.239) | copy-start | bytes 3076
  56.9 98.1 %copy-start.16 = (pred[1024]{0:T(1024)(128)(4,1)}, pred[1024]{0:T(1024)(128)(4,1)S(1)}, u32[]{:S(2)}) copy-start(pred[1024]{0:T(1024)(128)(4,1)S(1)} %get-tuple-element.240) | copy-start | bytes 3076
  61.5 4.6 collective-permute-start.11
  61.5 89.8 %copy-start.8 = (pred[1024]{0:T(1024)(128)(4,1)}, pred[1024]{0:T(1024)(128)(4,1)S(1)}, u32[]{:S(2)}) copy-start(pred[1024]{0:T(1024)(128)(4,1)S(1)} %get-tuple-element.241) | copy-start | bytes 3076
  61.5 91.0 %copy-start.10 = (pred[1024]{0:T(1024)(128)(4,1)}, pred[1024]{0:T(1024)(128)(4,1)S(1)}, u32[]{:S(2)}) copy-start(pred[1024]{0:T(1024)(128)(4,1)S(1)} %get-tuple-element.242) | copy-start | bytes 3076
  66.0 4.6 collective-permute-start.12
  66.0 82.8 %copy-start.4 = (pred[1024]{0:T(1024)(128)(4,1)}, pred[1024]{0:T(1024)(128)(4,1)S(1)}, u32[]{:S(2)}) copy-start(pred[1024]{0:T(1024)(128)(4,1)S(1)} %get-tuple-element.243) | copy-start | bytes 3076
  66.0 83.9 %copy-start.6 = (pred[1024]{0:T(1024)(128)(4,1)}, pred[1024]{0:T(1024)(128)(4,1)S(1)}, u32[]{:S(2)}) copy-start(pred[1024]{0:T(1024)(128)(4,1)S(1)} %get-tuple-element.244) | copy-start | bytes 3076
  70.6 4.5 collective-permute-start.13
  70.6 75.5 %copy-start.14 = (pred[1024]{0:T(1024)(128)(4,1)}, pred[1024]{0:T(1024)(128)(4,1)S(1)}, u32[]{:S(2)}) copy-start(pred[1024]{0:T(1024)(128)(4,1)S(1)} %get-tuple-element.245) | copy-start | bytes 3076
  70.6 76.9 %copy-start.2 = (pred[1024]{0:T(1024)(128)(4,1)}, pred[1024]{0:T(1024)(128)(4,1)S(1)}, u32[]{:S(2)}) copy-start(pred[1024]{0:T(1024)(128)(4,1)S(1)} %get-tuple-element.246) | copy-start | bytes 3076
  75.1 4.6 collective-permute-start.14
  75.1 69.7 %copy-start.19 = (pred[1024]{0:T(1024)(128)(4,1)}, pred[1024]{0:T(1024)(128)(4,1)S(1)}, u32[]{:S(2)}) copy-start(pred[1024]{0:T(1024)(128)(4,1)S(1)} %and_compare_fusion) | copy-start | bytes 3076
  150.0 10.7 %copy-start = (s32[16,1024]{1,0:T(8,128)S(1)}, s32[16,1024]{1,0:T(8,128)}, u32[]{:S(2)}) copy-start(s32[16,1024]{1,0:T(8,128)} %param.10) | copy-start | bytes 196612
  152.3 16.9 %copy-start.1 = (s32[10240]{0:T(1024)S(1)}, s32[10240]{0:T(1024)}, u32[]{:S(2)}) copy-start(s32[10240]{0:T(1024)} %param.12) | copy-start | bytes 122884
  156.6 12.1 %collective-permute-start.19 = (bf16[256,1024]{0,1:T(8,128)(2,1)S(1)}, bf16[256,1024]{0,1:T(8,128)(2,1)S(1)}, u32[]{:S(2)}, u32[]{:S(2)}) collective-permute-start(bf16[256,1024]{0,1:T(8,128)(2,1)S(1)} %get-tuple-element.21), channel_id=1, source_target_pairs={{0,1},{1,0},{2,3},{3,2},{4,5},{5,4},{6,7},{7,6},{8,9},{9,8},{10,11... | collective-permute-start | bytes 1572872 | tf_op jit(solution)/shard_map/ppermute | solution.py:10
  169.1 13.7 %collective-permute-start.20 = (bf16[256,1024]{0,1:T(8,128)(2,1)S(1)}, bf16[256,1024]{0,1:T(8,128)(2,1)S(1)}, u32[]{:S(2)}, u32[]{:S(2)}) collective-permute-start(bf16[256,1024]{0,1:T(8,128)(2,1)S(1)} %fusion.182), channel_id=1, source_target_pairs={{0,2},{1,3},{2,0},{3,1},{4,6},{5,7},{6,4},{7,5},{8,10},{9,11},{10,... | collective-permute-start | bytes 1572872 | tf_op jit(solution)/shard_map/ppermute | solution.py:10
  184.4 38.8 %copy-start.18 = (s32[1024]{0:T(1024)S(1)}, s32[1024]{0:T(1024)}, u32[]{:S(2)}) copy-start(s32[1024]{0:T(1024)} %get-tuple-element.225) | copy-start | bytes 12292
  184.4 36.6 %collective-permute-start.21 = (bf16[256,1024]{0,1:T(8,128)(2,1)}, bf16[256,1024]{0,1:T(8,128)(2,1)}, u32[]{:S(2)}, u32[]{:S(2)}) collective-permute-start(bf16[256,1024]{0,1:T(8,128)(2,1)} %get-tuple-element.18), channel_id=1, source_target_pairs={{0,4},{1,5},{2,6},{3,7},{4,0},{5,1},{6,2},{7,3},{8,12},{9,13},{10,... | collective-permute-start | bytes 1572872 | tf_op jit(solution)/shard_map/ppermute | solution.py:10
  209.4 188.5 %copy-start.17 = (pred[1024]{0:T(1024)(128)(4,1)S(1)}, pred[1024]{0:T(1024)(128)(4,1)}, u32[]{:S(2)}) copy-start(pred[1024]{0:T(1024)(128)(4,1)} %copy-done.16) | copy-start | bytes 3076
  209.4 61.6 %collective-permute-start.15 = (f32[256,1024]{0,1:T(8,128)}, f32[256,1024]{0,1:T(8,128)}, u32[]{:S(2)}, u32[]{:S(2)}) collective-permute-start(f32[256,1024]{0,1:T(8,128)} %fusion.3), channel_id=1, source_target_pairs={{0,8},{1,9},{2,10},{3,11},{4,12},{5,13},{6,14},{7,15},{8,0},{9,1},... | collective-permute-start | bytes 3145736 | tf_op jit(solution)/shard_map/ppermute | solution.py:10
  223.2 47.7 %collective-permute-start.22 = (bf16[256,1024]{0,1:T(8,128)(2,1)}, bf16[256,1024]{0,1:T(8,128)(2,1)}, u32[]{:S(2)}, u32[]{:S(2)}) collective-permute-start(bf16[256,1024]{0,1:T(8,128)(2,1)} %fusion.57), channel_id=1, source_target_pairs={{0,8},{1,9},{2,10},{3,11},{4,12},{5,13},{6,14},{7,15},{8,0},{9,1},... | collective-permute-start | bytes 1572872 | tf_op jit(solution)/shard_map/ppermute | solution.py:10
  270.9 129.2 %copy-start.13 = (pred[1024]{0:T(1024)(128)(4,1)S(1)}, pred[1024]{0:T(1024)(128)(4,1)}, u32[]{:S(2)}) copy-start(pred[1024]{0:T(1024)(128)(4,1)} %copy-done.12) | copy-start | bytes 3076
  273.7 61.2 %collective-permute-start.16 = (f32[256,1024]{0,1:T(8,128)S(1)}, f32[256,1024]{0,1:T(8,128)S(1)}, u32[]{:S(2)}, u32[]{:S(2)}) collective-permute-start(f32[256,1024]{0,1:T(8,128)S(1)} %get-tuple-element.17), channel_id=1, source_target_pairs={{0,4},{1,5},{2,6},{3,7},{4,0},{5,1},{6,2},{7,3},{8,12},{9,13},{10,... | collective-permute-start | bytes 3145736 | tf_op jit(solution)/shard_map/ppermute | solution.py:10
  335.2 24.3 %collective-permute-start.17 = (f32[256,1024]{0,1:T(8,128)S(1)}, f32[256,1024]{0,1:T(8,128)S(1)}, u32[]{:S(2)}, u32[]{:S(2)}) collective-permute-start(f32[256,1024]{0,1:T(8,128)S(1)} %multiply_subtract_fusion.11), channel_id=1, source_target_pairs={{0,2},{1,3},{2,0},{3,1},{4,6},{5,7},{6,4},{7,5},{8,10},{9,11},{10,... | collective-permute-start | bytes 3145736 | tf_op jit(solution)/shard_map/ppermute | solution.py:10
  361.6 33.4 %collective-permute-start.18 = (f32[256,1024]{0,1:T(8,128)}, f32[256,1024]{0,1:T(8,128)S(1)}, u32[]{:S(2)}, u32[]{:S(2)}) collective-permute-start(f32[256,1024]{0,1:T(8,128)} %get-tuple-element.20), channel_id=1, source_target_pairs={{0,1},{1,0},{2,3},{3,2},{4,5},{5,4},{6,7},{7,6},{8,9},{9,8},{10,11... | collective-permute-start | bytes 3145736 | tf_op jit(solution)/shard_map/ppermute | solution.py:10
  397.6 5.8 %copy-start.11 = (pred[1024]{0:T(1024)(128)(4,1)S(1)}, pred[1024]{0:T(1024)(128)(4,1)}, u32[]{:S(2)}) copy-start(pred[1024]{0:T(1024)(128)(4,1)} %copy-done.10) | copy-start | bytes 3076
  399.9 6.6 %copy-start.9 = (pred[1024]{0:T(1024)(128)(4,1)S(1)}, pred[1024]{0:T(1024)(128)(4,1)}, u32[]{:S(2)}) copy-start(pred[1024]{0:T(1024)(128)(4,1)} %copy-done.8) | copy-start | bytes 3076
  403.2 6.3 %copy-start.7 = (pred[1024]{0:T(1024)(128)(4,1)S(1)}, pred[1024]{0:T(1024)(128)(4,1)}, u32[]{:S(2)}) copy-start(pred[1024]{0:T(1024)(128)(4,1)} %copy-done.6) | copy-start | bytes 3076
  406.3 6.1 %copy-start.5 = (pred[1024]{0:T(1024)(128)(4,1)S(1)}, pred[1024]{0:T(1024)(128)(4,1)}, u32[]{:S(2)}) copy-start(pred[1024]{0:T(1024)(128)(4,1)} %copy-done.4) | copy-start | bytes 3076
  409.3 6.0 %copy-start.3 = (pred[1024]{0:T(1024)(128)(4,1)S(1)}, pred[1024]{0:T(1024)(128)(4,1)}, u32[]{:S(2)}) copy-start(pred[1024]{0:T(1024)(128)(4,1)} %copy-done.2) | copy-start | bytes 3076
  412.3 6.1 %copy-start.15 = (pred[1024]{0:T(1024)(128)(4,1)S(1)}, pred[1024]{0:T(1024)(128)(4,1)}, u32[]{:S(2)}) copy-start(pred[1024]{0:T(1024)(128)(4,1)} %copy-done.14) | copy-start | bytes 3076
  509.9 21.4 %all-to-all-start = ((f32[16,14,512]{2,1,0:T(8,128)}), f32[16,14,512]{2,1,0:T(8,128)}, u32[]{:S(2)}, u32[]{:S(2)}) async-start(f32[16,14,512]{2,1,0:T(8,128)} %bitcast.44), calls=%async_computation | async-start | bytes 1048576 | tf_op jit(solution)/shard_map/all_to_all | solution.py:21
  533.3 16.3 %all-to-all-start.1 = ((f32[16,14,512]{2,1,0:T(8,128)}), f32[16,14,512]{2,1,0:T(8,128)}, u32[]{:S(2)}, u32[]{:S(2)}) async-start(f32[16,14,512]{2,1,0:T(8,128)} %broadcast_in_dim.368), calls=%async_computation.1 | async-start | bytes 1048576 | tf_op jit(solution)/shard_map/all_to_all | solution.py:27
Sparse Core Ops, SparseCore 0:
  9.8 49.3 all-gather.4
  61.6 135.1 all-gather.2
